TPU v7x, 256 devices: a whole 4x4x8 slice. The times are simulated.
256 devices in a mesh: pipe: 8 (over z), section: 4 (over y_hi, core), tensor: 8 (over x, y_lo).
Axes of the slice: x: 4, y: 4 (y_hi: 2, y_lo: 2; y = y_hi * 2 + y_lo), z: 8, core: 2. Of those that a mesh axis runs over, the one named last changes fastest.
Arguments:
- tokens: bfloat16 [8, 4, 2, 256, 8192], P('pipe', 'section', None, None, 'tensor'), may hold values from -51 to 51
- norm_gain: bfloat16 [4, 8192], P('section', 'tensor'), may hold values from 0.25 to 1.75
- held_kv: bfloat16 [4, 8192, 2048], P('section', 'tensor', 'pipe'), may hold values from -0.0625 to 0.0625
- block_holder: int32 [4, 8], replicated, may hold values from 0 to 7, each once within a row
- section_layer: int32 [8, 4], replicated, may hold values from 0 to 3, each once within a row
- cotangent: bfloat16 [8, 4, 2, 256, 2048], P('pipe', 'section', None, None, 'tensor'), may hold values from -6 to 6
Outputs:
- keys_values: bfloat16 [8, 4, 2, 256, 2048], P('pipe', 'section', None, None, 'tensor')
- token_grad: bfloat16 [8, 4, 2, 256, 8192], P('pipe', 'section', None, None, 'tensor')
- kv_grads: bfloat16 [4, 8192, 2048], P('section', 'tensor', 'pipe')
Inputs may be any that keep to these rules, and one draw needn't show every extreme that they name: Each row of section_layer is a permutation of the 4 window layers. Each row of block_holder is a permutation of the 8 relays.
All inputs are finite; a program needn't handle non-finite values.
Results may differ from a plain program's by a relative error of at most 0.0057.
Values may be sent and summed in bfloat16 or wider, within the bound.
No kernel may reach another device: no remote copies, remote signals or barrier semaphores. Data moves between devices by JAX's collectives and lax.ppermute only.
A program may use at most 128 MiB of HBM per device.

v0:
```python
import jax
import jax.numpy as jnp
from jax import lax
from jax.sharding import PartitionSpec as P

D = 8192
EPSILON = 1e-05


def invert_slots(holder_row):
    slot_count = holder_row.shape[0]
    slot_ids = jnp.arange(slot_count, dtype=jnp.int32)
    slot_match = holder_row[None, :] == slot_ids[:, None]
    return jnp.sum(jnp.where(slot_match, slot_ids[None, :], 0), axis=1)


def per_device(tokens, norm_gain, held_kv, block_holder, section_layer, cotangent):
    pipe_index = lax.axis_index("pipe")
    section_index = lax.axis_index("section")
    pipe_count = lax.axis_size("pipe")
    section_count = lax.axis_size("section")
    layer_index = section_layer[pipe_index, section_index]
    every_block, every_gain = (
        lax.all_gather(held_kv, ("pipe", "section"), axis=0, tiled=True),
        lax.all_gather(norm_gain, ("pipe", "section"), axis=0, tiled=True),
    )
    sources = jnp.arange(pipe_count, dtype=jnp.int32) * section_count + layer_index
    my_blocks = jnp.take(every_block, sources, axis=0)
    layer_gain = every_gain[layer_index]
    weight_blocks = jnp.take(my_blocks, block_holder[layer_index], axis=0)
    gain_f32 = layer_gain.astype(jnp.float32)
    micro_count = tokens.shape[2]
    tok_count = tokens.shape[3]
    feat_local = tokens.shape[4]
    row_count = micro_count * tok_count
    inputs = tokens.reshape(row_count, feat_local).astype(jnp.float32)
    squares = lax.psum(jnp.sum(inputs * inputs, axis=1), "tensor")
    scale_rows = lax.rsqrt(squares / D + EPSILON)
    normed = (inputs * scale_rows[:, None] * gain_f32).astype(jnp.bfloat16)
    partial_kv = jnp.einsum(
        "rd,bdc->rbc", normed, weight_blocks, preferred_element_type=jnp.float32
    ).reshape(row_count, -1)
    kv_local = lax.psum_scatter(partial_kv, "tensor", scatter_dimension=1, tiled=True)
    keys_values = kv_local.astype(jnp.bfloat16).reshape(1, 1, micro_count, tok_count, -1)
    upstream_local = cotangent.reshape(row_count, -1)
    upstream = lax.all_gather(upstream_local, "tensor", axis=1, tiled=True)
    upstream_blocks = upstream.reshape(row_count, pipe_count, -1)
    normed_grad = jnp.einsum(
        "rbc,bdc->rd", upstream_blocks, weight_blocks, preferred_element_type=jnp.float32
    )
    grad_blocks = jnp.einsum(
        "rd,rbc->bdc", normed, upstream_blocks, preferred_element_type=jnp.float32
    ).astype(jnp.bfloat16)
    outgoing_grads = jnp.take(grad_blocks, invert_slots(block_holder[layer_index]), axis=0)
    arrived = lax.all_to_all(outgoing_grads, "pipe", split_axis=0, concat_axis=0, tiled=True)
    layer_ids = jnp.arange(section_count, dtype=jnp.int32)
    owner_table = (section_layer[:, section_index][None, :] == layer_ids[:, None]).astype(
        jnp.bfloat16
    )
    per_layer = jnp.einsum("lq,qdc->ldc", owner_table, arrived, preferred_element_type=jnp.float32)
    summed = lax.psum_scatter(per_layer, "section", scatter_dimension=0, tiled=True)
    kv_grads = summed.astype(jnp.bfloat16)
    row_inner = lax.psum(jnp.sum(gain_f32 * normed_grad * inputs, axis=1), "tensor")
    token_grad = (
        scale_rows[:, None] * gain_f32 * normed_grad
        - inputs * (scale_rows**3 * row_inner / D)[:, None]
    ).astype(jnp.bfloat16)
    return (keys_values, token_grad.reshape(tokens.shape), kv_grads)


def solution(mesh):
    placed = (
        P("pipe", "section", None, None, "tensor"),
        P("section", "tensor"),
        P("section", "tensor", "pipe"),
        P(),
        P(),
        P("pipe", "section", None, None, "tensor"),
    )
    return jax.shard_map(
        per_device,
        mesh=mesh,
        in_specs=placed,
        out_specs=(
            P("pipe", "section", None, None, "tensor"),
            P("pipe", "section", None, None, "tensor"),
            P("section", "tensor", "pipe"),
        ),
        check_vma=False,
    )
```

profile of v0, /device:TPU:1, one launch (start us, length us, event | category | flops | bytes accessed | tf_op | source)
XLA Modules:
  0.0 425.6 jit_solution(6199539240854835074)
XLA Ops:
  7.2 0.0 all-gather.4.cloned.1.call-start
  7.2 0.7 all-gather.4.cloned.1.call-update
  7.9 0.0 all-gather.6.cloned.1.call-start
  7.9 1.8 copy.39
  9.7 0.0 all-gather.6.cloned.1.call-update
  9.8 0.0 reduce-scatter.3.cloned.1.call-start
  9.8 1.3 dynamic_slice.13
  14.3 1.5 fusion.6
  15.8 46.9 %all-gather = bf16[32,1,1024]{2,1,0:T(2,128)(2,1)S(1)} all-gather(bf16[1,1,1024]{2,1,0:T(2,128)(2,1)} %bitcast.61), channel_id=1, replica_groups=mesh['pipe'=8,'section'=4,'tensor'=8] {'pipe','section'}, dimensions={0}, use_global_device_ids=true | all-gather | bytes 67584 | tf_op jit(solution)/shard_map/all_gather | solution.py:25
  62.8 0.7 fusion.18
  63.4 0.7 compare_and_fusion.2
  64.1 0.7 compare_and_fusion.1
  64.8 0.1 select_reduce_fusion
  65.0 87.9 %all-gather.4.cloned.1.call-done = bf16[32,1024,256]{2,1,0:T(8,128)(2,1)} async-done(((bf16[1,1024,256]{2,1,0:T(8,128)(2,1)}), bf16[32,1024,256]{2,1,0:T(8,128)(2,1)}) %all-gather.4.cloned.1.call-update) | async-done | bytes 16777232 | tf_op jit(solution)/shard_map/all_gather | solution.py:24
  152.9 8.5 %gather_fusion = bf16[8,1024,256]{2,1,0:T(8,128)(2,1)} fusion(bf16[32,1024,256]{2,1,0:T(8,128)(2,1)} %all-gather.4.cloned.1.call-done, s32[1024]{0:T(1024)S(1)} %pad_clamp_fusion.2), kind=kCustom, calls=%fused_computation.2 | custom fusion | bytes 8388640 | tf_op jit(solution)/shard_map/jit(_take)/gather | solution.py:28
  161.4 4.7 %broadcast_select_fusion.2 = bf16[8,1024,256]{2,1,0:T(8,128)(2,1)} fusion(bf16[8,1024,256]{2,1,0:T(8,128)(2,1)} %gather_fusion, pred[8]{0:T(512)(128)(4,1)S(1)} %compare_and_fusion.2), kind=kLoop, calls=%fused_computation.8 | loop fusion | flops 2097152 | bytes 8388616 | tf_op jit(solution)/shard_map/jit(_take)/select_n | solution.py:28
  166.1 4.9 %gather_fusion.1 = bf16[8,1024,256]{2,1,0:T(8,128)(2,1)} fusion(bf16[8,1024,256]{2,1,0:T(8,128)(2,1)} %broadcast_select_fusion.2, s32[1024]{0:T(1024)S(1)} %pad_clamp_fusion.1), kind=kCustom, calls=%fused_computation.clone | custom fusion | bytes 8388640 | tf_op jit(solution)/shard_map/jit(_take)/gather | solution.py:30
  171.0 0.0 copy-start
  171.0 4.7 %fusion.10 = bf16[8,256,1024]{1,2,0:T(8,128)(2,1)} fusion(bf16[8,1024,256]{2,1,0:T(8,128)(2,1)} %gather_fusion.1, pred[8]{0:T(512)(128)(4,1)S(1)} %get-tuple-element.15), kind=kLoop, calls=%fused_computation.22 | loop fusion | flops 2097152 | bytes 8388616 | tf_op jit(solution)/shard_map/rd,bdc->rbc/dot_general | solution.py:40
  175.7 28.8 %all-gather.6.cloned.1.call-done = bf16[512,2048]{0,1:T(8,128)(2,1)} async-done(((bf16[512,256]{0,1:T(8,128)(2,1)}), bf16[512,2048]{0,1:T(8,128)(2,1)}) %all-gather.6.cloned.1.call-update) | async-done | bytes 2097168 | tf_op jit(solution)/shard_map/all_gather | solution.py:46
  204.5 0.0 copy-done
  204.5 5.4 %fusion.5 = (f32[512]{0:T(512)S(1)}, f32[1024,512,1]{0,1,2:T(8,128)S(1)}) fusion(bf16[1,1,2,256,1024]{4,3,2,1,0:T(8,128)(2,1)S(1)} %copy-done, f32[1024]{0:T(1024)S(1)} %bitcast.56, bf16[512,8,256]{0,2,1:T(8,128)(2,1)} %bitcast.62, bf16[8,1024,256]{2,1,0:T(8,128)(2,1)} %gather_fusion.1, pred[8]{0:T(512)(128)(4,1)S(1)} %get-tuple-element.15), kind=kOutput, calls=%fused_computation.14 | convolution fusion | flops 2151677440 | bytes 9443336 | tf_op jit(solution)/shard_map/rbc,bdc->rd/dot_general | solution.py:48
  209.9 14.6 %all-reduce = (f32[512]{0:T(512)S(1)}, f32[512]{0:T(512)S(1)}) all-reduce(f32[512]{0:T(512)S(1)} %bitcast.60, f32[512]{0:T(512)S(1)} %get-tuple-element.19), channel_id=1, replica_groups=mesh['pipe'=8,'section'=4,'tensor'=8] {'tensor'}, use_global_device_ids=true, to_apply=%region_1.2 | all-reduce | flops 1024 | bytes 8192 | tf_op jit(solution)/shard_map/psum | solution.py:37
  224.6 1.3 fusion.8
  225.8 6.5 %copy.29 = bf16[8,256,1024]{2,1,0:T(8,128)(2,1)} copy(bf16[8,256,1024]{1,2,0:T(8,128)(2,1)} %fusion.10) | data formatting | bytes 8388608 | tf_op jit(solution)/shard_map/rd,bdc->rbc/dot_general | solution.py:40
  232.3 6.8 %fusion.21 = f32[512,2048]{1,0:T(8,128)} fusion(bf16[512,1024]{1,0:T(8,128)(2,1)} %bitcast.51, bf16[2048,1024]{1,0:T(8,128)(2,1)} %bitcast.50), kind=kOutput, calls=%fused_computation.49 | convolution fusion | flops 2147483648 | bytes 9437184 | tf_op jit(solution)/shard_map/rd,bdc->rbc/dot_general | solution.py:40
  239.1 0.0 reduce-scatter.3.cloned.1.call-update
  239.2 6.3 %convert_bitcast_fusion = bf16[8,1024,256]{2,1,0:T(8,128)(2,1)} fusion(bf16[512,1024,1]{1,0,2:T(8,128)(2,1)} %bitcast.52, bf16[512,8,256]{0,2,1:T(8,128)(2,1)} %bitcast.63), kind=kOutput, calls=%fused_computation.5 | convolution fusion | flops 2149580800 | bytes 7340032 | tf_op jit(solution)/shard_map/rd,rbc->bdc/dot_general | solution.py:51
  245.4 5.0 %gather_fusion.2 = bf16[8,1024,256]{2,1,0:T(8,128)(2,1)} fusion(bf16[8,1024,256]{2,1,0:T(8,128)(2,1)} %convert_bitcast_fusion, s32[1024]{0:T(1024)S(1)} %pad_clamp_fusion), kind=kCustom, calls=%fused_computation.1.clone | custom fusion | bytes 8388640 | tf_op jit(solution)/shard_map/jit(_take)/gather | solution.py:54
  250.4 4.6 %broadcast_select_fusion = bf16[8,1024,256]{2,1,0:T(8,128)(2,1)} fusion(bf16[8,1024,256]{2,1,0:T(8,128)(2,1)} %gather_fusion.2, pred[8]{0:T(512)(128)(4,1)S(1)} %compare_and_fusion), kind=kLoop, calls=%fused_computation.6 | loop fusion | flops 2097152 | bytes 8388616 | tf_op jit(solution)/shard_map/jit(_take)/select_n | solution.py:54
  255.0 7.2 %all-to-all-start = ((bf16[8,1024,256]{2,1,0:T(8,128)(2,1)}), bf16[8,1024,256]{2,1,0:T(8,128)(2,1)}, u32[]{:S(2)}, u32[]{:S(2)}) async-start(bf16[8,1024,256]{2,1,0:T(8,128)(2,1)} %broadcast_select_fusion), calls=%async_computation.1 | async-start | bytes 8388608 | tf_op jit(solution)/shard_map/all_to_all | solution.py:55
  262.3 0.2 reduce-scatter.5.cloned.1.call-start
  262.5 0.7 fusion.17
  263.2 90.4 %all-to-all-done = bf16[8,1024,256]{2,1,0:T(8,128)(2,1)} async-done(((bf16[8,1024,256]{2,1,0:T(8,128)(2,1)}), bf16[8,1024,256]{2,1,0:T(8,128)(2,1)}, u32[]{:S(2)}, u32[]{:S(2)}) %all-to-all-start) | async-done | bytes 4194336 | tf_op jit(solution)/shard_map/all_to_all | solution.py:55
  353.6 4.9 %fusion = f32[4,1024,256]{2,0,1:T(4,128)S(1)} fusion(bf16[8,1024,256]{2,1,0:T(8,128)(2,1)} %all-to-all-done, s32[8]{0:T(128)S(1)} %fusion.17), kind=kOutput, calls=%fused_computation.3 | convolution fusion | flops 16777248 | bytes 8388640 | tf_op jit(solution)/shard_map/lq,qdc->ldc/dot_general | solution.py:60
  358.5 2.7 copy.35
  361.2 0.0 reduce-scatter.5.cloned.1.call-update
  361.3 1.4 fusion.3
  362.7 0.0 reduce-scatter.3.cloned.1.call-done
  362.7 1.8 convert_element_type.39
  364.5 52.6 %reduce-scatter.5.cloned.1.call-done = f32[1,1024,256]{2,1,0:T(8,128)} async-done(((f32[4,1024,256]{2,1,0:T(8,128)}), f32[1,1024,256]{2,1,0:T(8,128)}) %reduce-scatter.5.cloned.1.call-update) | async-done | bytes 1048592 | tf_op jit(solution)/shard_map/reduce_scatter | solution.py:61
  417.0 2.1 convert_element_type.45
  (10 shorter events, 0.1 us)
Async XLA Ops:
  7.2 145.7 %all-gather.4.cloned.1.call-start = ((), (), s32[]{:S(2)}) async-start(), calls=%async_computation.3 | async-start | bytes 17301504 | tf_op jit(solution)/shard_map/all_gather | solution.py:24
  7.9 196.6 %all-gather.6.cloned.1.call-start = ((), (), s32[]{:S(2)}) async-start(), calls=%async_computation.5 | async-start | bytes 2359296 | tf_op jit(solution)/shard_map/all_gather | solution.py:46
  9.8 352.9 %reduce-scatter.3.cloned.1.call-start = ((), (), s32[]{:S(2)}) async-start(), calls=%async_computation.4 | async-start | bytes 4718592 | tf_op jit(solution)/shard_map/reduce_scatter | solution.py:43
  171.0 33.5 %copy-start = (bf16[1,1,2,256,1024]{4,3,2,1,0:T(8,128)(2,1)S(1)}, bf16[1,1,2,256,1024]{4,3,2,1,0:T(8,128)(2,1)}, u32[]{:S(2)}) copy-start(bf16[1,1,2,256,1024]{4,3,2,1,0:T(8,128)(2,1)} %param.8) | copy-start | bytes 3145732
  255.0 98.6 %all-to-all-start = ((bf16[8,1024,256]{2,1,0:T(8,128)(2,1)}), bf16[8,1024,256]{2,1,0:T(8,128)(2,1)}, u32[]{:S(2)}, u32[]{:S(2)}) async-start(bf16[8,1024,256]{2,1,0:T(8,128)(2,1)} %broadcast_select_fusion), calls=%async_computation.1 | async-start | bytes 8388608 | tf_op jit(solution)/shard_map/all_to_all | solution.py:55
  262.3 154.8 %reduce-scatter.5.cloned.1.call-start = ((), (), s32[]{:S(2)}) async-start(), calls=%async_computation.6 | async-start | bytes 5242880 | tf_op jit(solution)/shard_map/reduce_scatter | solution.py:61
Sparse Core Ops, SparseCore 0:
  10.8 142.0 all-gather.3
  155.3 49.2 all-gather.5
  239.3 95.7 reduce-scatter.2
  361.4 55.5 reduce-scatter.4
where the time goes:
time: 426 us
  waiting for transfers between devices  260 us (61%)
  blocking collectives  61.5 us (14%)
  local copies, waits for them, and re-layouts  31.4 us (7%)
  other arithmetic  24.2 us (6%)
  matrix products  23.4 us (5%)
  between operations  17.1 us (4%)
  starting transfers between devices  7.58 us (2%)
    all_to_all x1, waiting for transfers between devices, per_device(): lax.all_to_all(outgoing_grads, 'pipe', split_axis=0, concat_axis=0, tiled...  90.4 us
    all_gather x1, waiting for transfers between devices, per_device(): lax.all_gather(held_kv, ('pipe', 'section'), axis=0, tiled=True)  87.9 us
    reduce_scatter x1, waiting for transfers between devices, per_device(): lax.psum_scatter(per_layer, 'section', scatter_dimension=0, tiled=True)  52.6 us
    all_gather x1, blocking collectives, per_device(): lax.all_gather(norm_gain, ('pipe', 'section'), axis=0, tiled=True)  46.9 us
    all_gather x1, waiting for transfers between devices, per_device(): upstream = lax.all_gather(upstream_local, 'tensor', axis=1, tiled=True)  28.8 us
    psum x1, blocking collectives, per_device(): squares = lax.psum(jnp.sum(inputs * inputs, axis=1), 'tensor')  14.6 us
  transfers between devices with their start and end apart: 5, of which 4 were waited for; matrix products, arithmetic and copies ran while one was open for 13% of the time, Pallas kernels for 0%

commit v1 on v0

--- a/solution.py
+++ b/solution.py
@@ -20,8 +20,17 @@
     pipe_count = lax.axis_size("pipe")
     section_count = lax.axis_size("section")
     layer_index = section_layer[pipe_index, section_index]
+
+    def guide_lines_over_axis(q_in):
+        return jnp.concatenate(
+            lax.all_to_all(
+                jnp.stack([q_in] * lax.axis_size(("pipe", "section"))), ("pipe", "section"), 0, 0
+            ),
+            0,
+        )
+
     every_block, every_gain = (
-        lax.all_gather(held_kv, ("pipe", "section"), axis=0, tiled=True),
+        guide_lines_over_axis(held_kv),
         lax.all_gather(norm_gain, ("pipe", "section"), axis=0, tiled=True),
     )
     sources = jnp.arange(pipe_count, dtype=jnp.int32) * section_count + layer_index

time: 426 us -> 668 us (1.57)
  blocking collectives: 61.5 us -> 404 us
  waiting for transfers between devices: 260 us -> 143 us
  starting transfers between devices: 7.58 us -> 20.3 us
    all_gather x1, blocking collectives: 46.9 us -> 389 us  [per_device(): lax.all_gather(norm_gain, ('pipe', 'section'), axis=0, tiled=True)]
    all_gather x1 -> x0, waiting for transfers between devices: 87.9 us -> none  [per_device(): lax.all_gather(held_kv, ('pipe', 'section'), axis=0, tiled=True)]
    all_gather x1, waiting for transfers between devices: 28.8 us -> 0.01 us  [per_device(): upstream = lax.all_gather(upstream_local, 'tensor', axis=1, tiled=True)]
    all_to_all x0 -> x1, starting transfers between devices: none -> 13 us  [guide_lines_over_axis(): lax.all_to_all(jnp.stack([q_in] * lax.axis_size(('pipe', 'section'))), ('...]
    another operation x0 -> x1, local copies, waits for them, and re-layouts: none -> 6.75 us  [guide_lines_over_axis(): jnp.stack([q_in] * lax.axis_size(('pipe', 'section')))]
  transfers between devices with their start and end apart: 5 -> 5, of which waited for: 4 -> 2; matrix products, arithmetic and copies ran while one was open for 13% -> 8% of each run, Pallas kernels for 0% -> 0%
where the time goes in v1:
time: 668 us; the launch traced here: 667 us
  blocking collectives  404 us (60%)
  waiting for transfers between devices  143 us (21%)
  local copies, waits for them, and re-layouts  35.9 us (5%)
  matrix products  23.5 us (4%)
  other arithmetic  23.2 us (3%)
  starting transfers between devices  20.3 us (3%)
  between operations  17.1 us (3%)
    all_gather x1, blocking collectives, per_device(): lax.all_gather(norm_gain, ('pipe', 'section'), axis=0, tiled=True)  389 us
    all_to_all x1, waiting for transfers between devices, per_device(): lax.all_to_all(outgoing_grads, 'pipe', split_axis=0, concat_axis=0, tiled...  91.5 us
    reduce_scatter x1, waiting for transfers between devices, per_device(): lax.psum_scatter(per_layer, 'section', scatter_dimension=0, tiled=True)  51 us
    psum x1, blocking collectives, per_device(): squares = lax.psum(jnp.sum(inputs * inputs, axis=1), 'tensor')  15 us
  transfers between devices with their start and end apart: 5, of which 2 were waited for; matrix products, arithmetic and copies ran while one was open for 8% of the time, Pallas kernels for 0%

profile of v1, /device:TPU:1, one launch (start us, length us, event | category | flops | bytes accessed | tf_op | source)
XLA Modules:
  0.0 666.9 jit_solution(282979921165631776)
XLA Ops:
  7.2 6.8 %stack.2 = bf16[32,1,1024,256]{3,2,1,0:T(8,128)(2,1)} broadcast(bf16[1024,256]{1,0:T(8,128)(2,1)} %bitcast.56), dimensions={2,3} | broadcast | bytes 17301504 | tf_op jit(solution)/shard_map/stack | solution.py:27
  13.9 0.0 copy-start.1
  13.9 0.0 copy-start.3
  13.9 0.0 copy-start
  13.9 0.0 copy-start.2
  13.9 13.0 %all-to-all-start = ((bf16[32,1,1024,256]{3,2,1,0:T(8,128)(2,1)}), bf16[32,1,1024,256]{3,2,1,0:T(8,128)(2,1)}, u32[]{:S(2)}, u32[]{:S(2)}) async-start(bf16[32,1,1024,256]{3,2,1,0:T(8,128)(2,1)} %stack.2), calls=%async_computation | async-start | bytes 33554432 | tf_op jit(solution)/shard_map/all_to_all | solution.py:26
  26.9 0.0 all-gather.3.cloned.1.call-start
  26.9 0.0 copy-done.1
  27.0 0.8 copy.39
  27.8 0.0 all-gather.3.cloned.1.call-update
  27.8 0.0 reduce-scatter.3.cloned.1.call-start
  27.9 0.0 copy-done.3
  27.9 0.6 dynamic_slice.13
  31.7 0.0 copy-done
  31.7 0.3 fusion.6
  32.0 0.0 copy-done.2
  32.0 389.3 %all-gather = bf16[32,1,1024]{2,1,0:T(2,128)(2,1)S(1)} all-gather(bf16[1,1,1024]{2,1,0:T(2,128)(2,1)S(1)} %bitcast.64), channel_id=1, replica_groups=mesh['pipe'=8,'section'=4,'tensor'=8] {'pipe','section'}, dimensions={0}, use_global_device_ids=true | all-gather | bytes 67584 | tf_op jit(solution)/shard_map/all_gather | solution.py:34
  421.3 0.7 fusion.18
  422.0 0.7 compare_and_fusion.2
  422.6 0.7 compare_and_fusion.1
  423.4 0.1 select_reduce_fusion
  423.5 0.0 all-to-all-done
  423.5 8.5 %gather_fusion = bf16[8,1024,256]{2,1,0:T(8,128)(2,1)} fusion(bf16[32,1024,256]{2,1,0:T(8,128)(2,1)} %bitcast.6, s32[1024]{0:T(1024)S(1)} %pad_clamp_fusion.2), kind=kCustom, calls=%fused_computation.2 | custom fusion | bytes 8388640 | tf_op jit(solution)/shard_map/jit(_take)/gather | solution.py:37
  432.1 4.6 broadcast_select_fusion.2
  436.7 4.9 gather_fusion.1
  441.6 4.6 fusion.10
  446.2 0.0 all-gather.3.cloned.1.call-done
  446.2 5.4 fusion.5
  451.6 15.0 %all-reduce = (f32[512]{0:T(512)S(1)}, f32[512]{0:T(512)S(1)}) all-reduce(f32[512]{0:T(512)S(1)} %bitcast.63, f32[512]{0:T(512)S(1)} %get-tuple-element.19), channel_id=1, replica_groups=mesh['pipe'=8,'section'=4,'tensor'=8] {'tensor'}, use_global_device_ids=true, to_apply=%region_1.2 | all-reduce | flops 1024 | bytes 8192 | tf_op jit(solution)/shard_map/psum | solution.py:46
  466.7 1.3 fusion.8
  468.0 6.5 copy.29
  474.5 6.8 %fusion.21 = f32[512,2048]{1,0:T(8,128)} fusion(bf16[512,1024]{1,0:T(8,128)(2,1)} %bitcast.53, bf16[2048,1024]{1,0:T(8,128)(2,1)} %bitcast.52), kind=kOutput, calls=%fused_computation.49 | convolution fusion | flops 2147483648 | bytes 9437184 | tf_op jit(solution)/shard_map/rd,bdc->rbc/dot_general | solution.py:49
  481.3 0.0 reduce-scatter.3.cloned.1.call-update
  481.3 6.3 convert_bitcast_fusion
  487.6 4.9 gather_fusion.2
  492.6 5.0 broadcast_select_fusion
  497.5 7.1 %all-to-all-start.1 = ((bf16[8,1024,256]{2,1,0:T(8,128)(2,1)}), bf16[8,1024,256]{2,1,0:T(8,128)(2,1)}, u32[]{:S(2)}, u32[]{:S(2)}) async-start(bf16[8,1024,256]{2,1,0:T(8,128)(2,1)} %broadcast_select_fusion), calls=%async_computation.2 | async-start | bytes 8388608 | tf_op jit(solution)/shard_map/all_to_all | solution.py:64
  504.6 0.2 reduce-scatter.5.cloned.1.call-start
  504.8 91.5 %all-to-all-done.1 = bf16[8,1024,256]{2,1,0:T(8,128)(2,1)} async-done(((bf16[8,1024,256]{2,1,0:T(8,128)(2,1)}), bf16[8,1024,256]{2,1,0:T(8,128)(2,1)}, u32[]{:S(2)}, u32[]{:S(2)}) %all-to-all-start.1) | async-done | bytes 4194336 | tf_op jit(solution)/shard_map/all_to_all | solution.py:64
  596.4 4.9 fusion
  601.3 2.7 copy.35
  604.1 0.0 reduce-scatter.5.cloned.1.call-update
  604.1 1.4 fusion.3
  605.5 0.0 reduce-scatter.3.cloned.1.call-done
  605.5 1.8 convert_element_type.39
  607.3 51.0 %reduce-scatter.5.cloned.1.call-done = f32[1,1024,256]{2,1,0:T(8,128)} async-done(((f32[4,1024,256]{2,1,0:T(8,128)}), f32[1,1024,256]{2,1,0:T(8,128)}) %reduce-scatter.5.cloned.1.call-update) | async-done | bytes 1048592 | tf_op jit(solution)/shard_map/reduce_scatter | solution.py:70
  658.3 2.1 convert_element_type.45
  (11 shorter events, 0.1 us)
Async XLA Ops:
  13.9 13.0 %copy-start.1 = (bf16[1,1,2,256,256]{4,3,2,1,0:T(8,128)(2,1)S(1)}, bf16[1,1,2,256,256]{4,3,2,1,0:T(8,128)(2,1)}, u32[]{:S(2)}) copy-start(bf16[1,1,2,256,256]{4,3,2,1,0:T(8,128)(2,1)} %param.13) | copy-start | bytes 786436
  13.9 14.0 %copy-start.3 = (s32[8,4]{0,1:T(4,128)S(1)}, s32[8,4]{0,1:T(4,128)}, u32[]{:S(2)}) copy-start(s32[8,4]{0,1:T(4,128)} %param.12) | copy-start | bytes 388
  13.9 17.8 %copy-start = (bf16[1,1,2,256,1024]{4,3,2,1,0:T(8,128)(2,1)S(1)}, bf16[1,1,2,256,1024]{4,3,2,1,0:T(8,128)(2,1)}, u32[]{:S(2)}) copy-start(bf16[1,1,2,256,1024]{4,3,2,1,0:T(8,128)(2,1)} %param.8) | copy-start | bytes 3145732
  13.9 18.1 %copy-start.2 = (bf16[1,1024]{1,0:T(2,128)(2,1)S(1)}, bf16[1,1024]{1,0:T(2,128)(2,1)}, u32[]{:S(2)}) copy-start(bf16[1,1024]{1,0:T(2,128)(2,1)} %param.9) | copy-start | bytes 6148
  13.9 409.6 %all-to-all-start = ((bf16[32,1,1024,256]{3,2,1,0:T(8,128)(2,1)}), bf16[32,1,1024,256]{3,2,1,0:T(8,128)(2,1)}, u32[]{:S(2)}, u32[]{:S(2)}) async-start(bf16[32,1,1024,256]{3,2,1,0:T(8,128)(2,1)} %stack.2), calls=%async_computation | async-start | bytes 33554432 | tf_op jit(solution)/shard_map/all_to_all | solution.py:26
  26.9 419.3 %all-gather.3.cloned.1.call-start = ((), (), s32[]{:S(2)}) async-start(), calls=%async_computation.5 | async-start | bytes 2359296 | tf_op jit(solution)/shard_map/all_gather | solution.py:55
  27.8 577.7 %reduce-scatter.3.cloned.1.call-start = ((), (), s32[]{:S(2)}) async-start(), calls=%async_computation.4 | async-start | bytes 4718592 | tf_op jit(solution)/shard_map/reduce_scatter | solution.py:52
  497.5 98.8 %all-to-all-start.1 = ((bf16[8,1024,256]{2,1,0:T(8,128)(2,1)}), bf16[8,1024,256]{2,1,0:T(8,128)(2,1)}, u32[]{:S(2)}, u32[]{:S(2)}) async-start(bf16[8,1024,256]{2,1,0:T(8,128)(2,1)} %broadcast_select_fusion), calls=%async_computation.2 | async-start | bytes 8388608 | tf_op jit(solution)/shard_map/all_to_all | solution.py:64
  504.6 153.7 %reduce-scatter.5.cloned.1.call-start = ((), (), s32[]{:S(2)}) async-start(), calls=%async_computation.6 | async-start | bytes 5242880 | tf_op jit(solution)/shard_map/reduce_scatter | solution.py:70
Sparse Core Ops, SparseCore 0:
  30.1 126.2 all-gather.2
  481.5 93.9 reduce-scatter.2
  604.2 54.0 reduce-scatter.4
